TPU v7x, 32 devices: a whole 2x2x4 slice. The times are simulated.
32 devices in a mesh: tau: 2 (over x), basis: 16 (over z, y, core).
Axes of the slice: x: 2, y: 2, z: 4, core: 2. Of those that a mesh axis runs over, the one named last changes fastest.
Arguments:
- three_center: bfloat16 [64, 512, 512], P(None, 'basis'), may hold values from -6 to 6
- tensor_mask: int32 [64, 32, 32], P(None, 'basis'), may hold values 0 or 1
- occupied_green: bfloat16 [1024, 512], P(('tau', 'basis')), parts along dimension 0, may hold values from -0.75 to 0.75
- occupied_mask: int32 [64, 32], P(('tau', 'basis')), parts along dimension 0, may hold values 0 or 1
- virtual_green: bfloat16 [1024, 512], P(('tau', 'basis')), parts along dimension 0, may hold values from -0.75 to 0.75
- virtual_mask: int32 [64, 32], P(('tau', 'basis')), parts along dimension 0, may hold values 0 or 1
- atom_size: int32 [32], replicated, may hold values from 8 to 16, as said below
- auxiliary_owner: int32 [64], replicated, may hold values from 0 to 63, each once
Outputs:
- chi_owned: float32 [128, 64], P(('tau', 'basis')), parts along dimension 0
There are 2 independent parts, one for each index of `tau`. A program takes and returns all parts, laid end to end along the dimension named above; an argument that names none is the same for every part. Nothing has to cross between parts.
Inputs may be any that keep to these rules, and one draw needn't show every extreme that they name: `atom_size`: each atom block holds 8 to 16 live functions; some block holds exactly 16 and some exactly 8. `auxiliary_owner`: A permutation of the auxiliary functions.
All inputs are finite; a program needn't handle non-finite values. No bound on the sum of `tensor_mask` or of `occupied_mask` or of `virtual_mask` on one device may be relied on, other than what follows from the above.
Results may differ from a plain program's by a relative error of at most 0.0041.
Values may be sent and summed in bfloat16 or wider, within the bound.
A program may use at most 128 MiB of HBM per device.

v0:
```python
import jax
import jax.numpy as jnp
from jax import lax
from jax.sharding import PartitionSpec as P

FA = 16


def expand_factor(block_mask, alive_rows, alive_cols):
    row_atoms = block_mask.shape[-2]
    col_atoms = block_mask.shape[-1]
    factor = (
        block_mask.astype(jnp.bfloat16)[..., :, None, :, None]
        * alive_rows.reshape(row_atoms, FA)[:, :, None, None]
        * alive_cols.reshape(col_atoms, FA)[None, None, :, :]
    )
    return factor.reshape(block_mask.shape[:-2] + (row_atoms * FA, col_atoms * FA))


def local(
    three_center,
    tensor_mask,
    occupied_green,
    occupied_mask,
    virtual_green,
    virtual_mask,
    atom_size,
    auxiliary_owner,
):
    panel_rows = occupied_green.shape[0]
    basis_total = occupied_green.shape[1]
    aux_count = auxiliary_owner.shape[0]
    device_place = lax.axis_index("basis")
    within = lax.iota(jnp.int32, FA)[None, :] < atom_size[:, None]
    alive_cols = within.astype(jnp.bfloat16).reshape(-1)
    alive_rows = lax.dynamic_slice_in_dim(alive_cols, device_place * panel_rows, panel_rows)
    occupied = occupied_green * expand_factor(occupied_mask, alive_rows, alive_cols)
    virtual = virtual_green * expand_factor(virtual_mask, alive_rows, alive_cols)
    masked_three = three_center * expand_factor(tensor_mask, alive_rows, alive_cols)
    inverse_order = (
        jnp.zeros((aux_count,), jnp.int32).at[auxiliary_owner].set(lax.iota(jnp.int32, aux_count))
    )
    ordered = jnp.take(masked_three, inverse_order, axis=0)
    slab_tensor = lax.all_to_all(ordered, "basis", split_axis=0, concat_axis=1, tiled=True)
    half_slab = jnp.einsum(
        "pns,ls->pnl",
        slab_tensor,
        lax.all_gather(virtual, "basis", axis=0, tiled=True),
        preferred_element_type=jnp.float32,
    ).astype(jnp.bfloat16)
    response_slab = jnp.einsum(
        "mn,pnl->pml",
        lax.all_gather(occupied, "basis", axis=0, tiled=True),
        half_slab,
        preferred_element_type=jnp.float32,
    ).astype(jnp.bfloat16)
    response_rows = lax.all_to_all(response_slab, "basis", split_axis=1, concat_axis=0, tiled=True)
    flat_three = ordered.reshape(aux_count, -1)
    flat_response = response_rows.reshape(aux_count, -1)
    chi_rows = lax.psum_scatter(
        jnp.einsum("ak,bk->ab", flat_three, flat_response, preferred_element_type=jnp.float32),
        "basis",
        scatter_dimension=0,
        tiled=True,
    )
    return jnp.take(chi_rows, auxiliary_owner, axis=1) * (1.0 / basis_total)


def solution(mesh):
    placed = (
        P(None, "basis", None),
        P(None, "basis", None),
        P(("tau", "basis"), None),
        P(("tau", "basis"), None),
        P(("tau", "basis"), None),
        P(("tau", "basis"), None),
        P(),
        P(),
    )
    return jax.shard_map(
        local, mesh=mesh, in_specs=placed, out_specs=P(("tau", "basis"), None), check_vma=False
    )
```

profile of v0, /device:TPU:0, one launch (start us, length us, event | category | flops | bytes accessed | tf_op | source)
XLA Modules:
  0.0 231.6 jit_solution(7246500346719335204)
XLA Ops:
  0.0 0.7 compare_select_fusion.1
  0.7 0.8 scatter_custom_fusion
  1.6 0.7 lt.63
  2.4 0.7 lt.59
  3.4 0.8 convert_element_type.32
  4.2 2.6 %mul.123 = bf16[64,2,16,32,16]{0,4,3,2,1:T(8,128)(2,1)} broadcast(bf16[64,2,16,32]{0,3,2,1:T(8,128)(2,1)S(1)} %broadcast_multiply_fusion), dimensions={0,1,2,3} | broadcast | bytes 2228224 | tf_op jit(solution)/shard_map/mul | solution.py:13
  6.8 4.7 %copy.25 = bf16[64,32,512]{2,1,0:T(8,128)(2,1)S(1)} copy(bf16[64,32,512]{0,2,1:T(8,128)(2,1)} %bitcast.34) | data formatting | bytes 4194304 | tf_op jit(solution)/shard_map/mul | solution.py:13
  11.5 3.1 %multiply_multiply_fusion = bf16[64,32,512]{2,1,0:T(8,128)(2,1)} fusion(bf16[64,32,512]{2,1,0:T(8,128)(2,1)} %param.8, bf16[64,32,512]{2,1,0:T(8,128)(2,1)S(1)} %copy.25, bf16[512]{0:T(512)(128)(2,1)S(1)} %get-tuple-element.5), kind=kLoop, calls=%fused_computation.6 | loop fusion | flops 2097152 | bytes 6292480 | tf_op jit(solution)/shard_map/mul | solution.py:39
  14.6 2.3 gather_fusion
  16.9 1.6 broadcast_select_fusion
  18.5 7.5 %all-to-all-start = ((bf16[64,32,512]{2,1,0:T(8,128)(2,1)}), bf16[64,32,512]{2,1,0:T(8,128)(2,1)S(1)}, u32[]{:S(2)}, u32[]{:S(2)}) async-start(bf16[64,32,512]{2,1,0:T(8,128)(2,1)} %broadcast_select_fusion), calls=%async_computation | async-start | bytes 4194304 | tf_op jit(solution)/shard_map/all_to_all | solution.py:44
  27.2 55.5 %all_gather.7 = bf16[512,512]{1,0:T(8,128)(2,1)S(1)} all-gather(bf16[32,512]{1,0:T(8,128)(2,1)S(1)} %get-tuple-element.8), channel_id=1, replica_groups=mesh['tau'=2,'basis'=16] {'basis'}, dimensions={0}, use_global_device_ids=true | all-gather | bytes 557056 | tf_op jit(solution)/shard_map/all_gather | solution.py:53
  82.7 24.0 %all_gather.6 = bf16[512,512]{1,0:T(8,128)(2,1)S(1)} all-gather(bf16[32,512]{1,0:T(8,128)(2,1)S(1)} %get-tuple-element.7), channel_id=1, replica_groups=mesh['tau'=2,'basis'=16] {'basis'}, dimensions={0}, use_global_device_ids=true | all-gather | bytes 557056 | tf_op jit(solution)/shard_map/all_gather | solution.py:48
  106.7 1.5 copy.26
  108.2 4.0 %convert_bitcast_fusion = bf16[4,512,512]{1,2,0:T(8,128)(2,1)S(1)} fusion(bf16[4,512,512]{2,1,0:T(8,128)(2,1)} %bitcast.40, bf16[512,512]{1,0:T(8,128)(2,1)S(1)} %all_gather.7, bf16[512,512]{1,0:T(8,128)(2,1)S(1)} %all_gather.6), kind=kOutput, calls=%fused_computation.3 | convolution fusion | flops 2149580800 | bytes 5242880 | tf_op jit(solution)/shard_map/mn,pnl->pml/dot_general | solution.py:51
  112.1 3.1 %copy.28 = bf16[4,512,512]{2,0,1:T(4,128)(2,1)} copy(bf16[4,512,512]{1,2,0:T(8,128)(2,1)S(1)} %convert_bitcast_fusion) | data formatting | bytes 4194304 | tf_op jit(solution)/shard_map/convert_element_type | solution.py:56
  115.2 3.7 %all-to-all-start.1 = ((bf16[4,512,512]{2,0,1:T(4,128)(2,1)}), bf16[4,512,512]{2,0,1:T(4,128)(2,1)S(1)}, u32[]{:S(2)}, u32[]{:S(2)}) async-start(bf16[4,512,512]{2,0,1:T(4,128)(2,1)} %copy.28), calls=%async_computation.1 | async-start | bytes 4194304 | tf_op jit(solution)/shard_map/all_to_all | solution.py:57
  119.0 4.2 %copy.34 = bf16[8,8,32,512]{3,1,2,0:T(8,128)(2,1)} copy(bf16[8,8,32,512]{3,2,1,0:T(8,128)(2,1)} %bitcast.14) | data formatting | bytes 4194304
  124.4 35.6 %all-to-all-done.1 = bf16[4,512,512]{2,0,1:T(4,128)(2,1)S(1)} async-done(((bf16[4,512,512]{2,0,1:T(4,128)(2,1)}), bf16[4,512,512]{2,0,1:T(4,128)(2,1)S(1)}, u32[]{:S(2)}, u32[]{:S(2)}) %all-to-all-start.1) | async-done | bytes 2097184 | tf_op jit(solution)/shard_map/all_to_all | solution.py:57
  160.7 1.3 copy.35
  162.2 0.7 fusion.11
  162.9 67.2 %all-reduce = f32[64,64]{1,0:T(8,128)S(1)} all-reduce(f32[64,64]{1,0:T(8,128)S(1)} %fusion.11), channel_id=2, replica_groups=mesh['tau'=2,'basis'=16] {'basis'}, use_global_device_ids=true, to_apply=%region_1.2.clone | all-reduce | flops 4096 | bytes 32768
  230.3 0.6 gather_fusion.1
  230.9 0.7 copy.32
  (43 shorter events, 3.4 us)
Async XLA Ops:
  18.5 7.5 %copy-start.3 = (s32[2,32]{1,0:T(2,128)S(1)}, s32[2,32]{1,0:T(2,128)}, u32[]{:S(2)}) copy-start(s32[2,32]{1,0:T(2,128)} %param.13) | copy-start | bytes 772
  18.5 7.6 %copy-start.4 = (s32[2,32]{1,0:T(2,128)S(1)}, s32[2,32]{1,0:T(2,128)}, u32[]{:S(2)}) copy-start(s32[2,32]{1,0:T(2,128)} %param.11) | copy-start | bytes 772
  18.5 8.7 %copy-start.1 = (bf16[32,512]{1,0:T(8,128)(2,1)S(1)}, bf16[32,512]{1,0:T(8,128)(2,1)}, u32[]{:S(2)}) copy-start(bf16[32,512]{1,0:T(8,128)(2,1)} %param.12) | copy-start | bytes 98308
  18.5 8.7 %copy-start.2 = (bf16[32,512]{1,0:T(8,128)(2,1)S(1)}, bf16[32,512]{1,0:T(8,128)(2,1)}, u32[]{:S(2)}) copy-start(bf16[32,512]{1,0:T(8,128)(2,1)} %param.10) | copy-start | bytes 98308
  18.5 88.2 %all-to-all-start = ((bf16[64,32,512]{2,1,0:T(8,128)(2,1)}), bf16[64,32,512]{2,1,0:T(8,128)(2,1)S(1)}, u32[]{:S(2)}, u32[]{:S(2)}) async-start(bf16[64,32,512]{2,1,0:T(8,128)(2,1)} %broadcast_select_fusion), calls=%async_computation | async-start | bytes 4194304 | tf_op jit(solution)/shard_map/all_to_all | solution.py:44
  115.2 44.8 %all-to-all-start.1 = ((bf16[4,512,512]{2,0,1:T(4,128)(2,1)}), bf16[4,512,512]{2,0,1:T(4,128)(2,1)S(1)}, u32[]{:S(2)}, u32[]{:S(2)}) async-start(bf16[4,512,512]{2,0,1:T(4,128)(2,1)} %copy.28), calls=%async_computation.1 | async-start | bytes 4194304 | tf_op jit(solution)/shard_map/all_to_all | solution.py:57
  119.0 4.2 %copy-start.6 = (u32[32]{0:T(128)S(1)}, u32[32]{0:T(128)}, u32[]{:S(2)}) copy-start(u32[32]{0:T(128)} %constant.47) | copy-start | bytes 388
  119.0 5.4 %copy-start.5 = (s32[64]{0:T(128)S(1)}, s32[64]{0:T(128)}, u32[]{:S(2)}) copy-start(s32[64]{0:T(128)} %param.15) | copy-start | bytes 772
  160.6 1.6 copy-start
where the time goes:
time: 232 us
  blocking collectives  147 us (63%)
  waiting for transfers between devices  35.6 us (15%)
  local copies, waits for them, and re-layouts  26.1 us (11%)
  starting transfers between devices  11.2 us (5%)
  other arithmetic  6.47 us (3%)
  matrix products  4.65 us (2%)
    unnamed x1, blocking collectives  67.2 us
    all_gather x1, blocking collectives, local(): lax.all_gather(occupied, 'basis', axis=0, tiled=True)  55.5 us
    all_to_all x1, waiting for transfers between devices, local(): lax.all_to_all(response_slab, 'basis', split_axis=1, concat_axis=0, tiled...  35.6 us
    all_gather x1, blocking collectives, local(): lax.all_gather(virtual, 'basis', axis=0, tiled=True)  24 us
    mul x7, local copies, waits for them, and re-layouts, expand_factor(): block_mask.astype(jnp.bfloat16)[..., :, None, :, None]  8.35 us
    all_to_all x1, starting transfers between devices, local(): lax.all_to_all(ordered, 'basis', split_axis=0, concat_axis=1, tiled=True)  7.53 us
    unnamed x18, local copies, waits for them, and re-layouts  6.36 us
  transfers between devices with their start and end apart: 2, of which 1 were waited for; matrix products, arithmetic and copies ran while one was open for 3% of the time, Pallas kernels for 0%

commit v1 on v0

v1 whole, which is shorter than its diff:
```python
import functools

import jax
import jax.numpy as jnp
from jax import lax
from jax.experimental import pallas as pl
from jax.experimental.pallas import tpu as pltpu
from jax.sharding import PartitionSpec as P

FA = 16
LANES = 128
GROUPS = 4
BF = jnp.bfloat16
F32 = jnp.float32


def wait_for(ref, sem):
    pltpu.make_async_copy(ref, ref, sem).wait()


def one_hot(cond):
    return jnp.where(cond, 1.0, 0.0).astype(F32)


def kernel(
    n,
    t_hbm,
    tmask_ref,
    og_ref,
    om_ref,
    vg_ref,
    vm_ref,
    size_ref,
    owner_ref,
    out_ref,
    tm,
    st,
    sh,
    rt,
    rh,
    vf,
    of,
    vt,
    perm,
    factor,
    chi,
    route,
    csend,
    crecv,
    load_sem,
    own_sem,
    small_send,
    small_recv,
    t_send,
    t_recv,
    h_send,
    h_recv,
    c_send,
    c_recv,
):
    me = lax.axis_index("basis")
    tau = lax.axis_index("tau")
    aux, width, basis = tm.shape
    pack = LANES // width
    groups = aux // pack
    steps = groups // GROUPS
    chunks = basis // LANES
    atoms = basis // FA
    row_atoms = width // FA
    wide = pack * LANES
    block_rows = GROUPS * width
    owned = aux // n
    pad_rows = csend.shape[1]

    def peer_of(k):
        return lax.rem(me + k, n)

    def each_peer(body):
        def step(k, carry):
            body(peer_of(k))
            return carry

        lax.fori_loop(1, n, step, 0)

    def target(peer):
        return dict(device_id=(tau, peer), device_id_type=pl.DeviceIdType.MESH)

    barrier = pltpu.get_barrier_semaphore()
    each_peer(lambda peer: pl.semaphore_signal(barrier, inc=1, **target(peer)))
    load = pltpu.make_async_copy(t_hbm, tm, load_sem)
    load.start()

    lane = lax.broadcasted_iota(jnp.int32, (1, basis), 1)
    live = jnp.zeros((1, basis), F32)
    for a in range(atoms):
        hit = (lane >= a * FA) & (lane < a * FA + size_ref[a])
        live = live + one_hot(hit)
    atom_row = lax.broadcasted_iota(jnp.int32, (atoms, basis), 0)
    atom_lane = lax.broadcasted_iota(jnp.int32, (atoms, basis), 1) // FA
    spread = (one_hot(atom_row == atom_lane) * live).astype(BF)
    within = lax.broadcasted_iota(jnp.int32, (FA, basis), 0)
    live_rows = [one_hot(within < size_ref[me * row_atoms + a]) for a in range(row_atoms)]

    def factors(mask):
        return jnp.dot(mask.astype(F32).astype(BF), spread, preferred_element_type=F32)

    def masked_rows(rows_ref, mask_ref):
        f = factors(mask_ref[...])
        parts = [
            rows_ref[a * FA : (a + 1) * FA, :].astype(F32) * (f[a : a + 1, :] * live_rows[a])
            for a in range(row_atoms)
        ]
        return jnp.concatenate(parts, axis=0).astype(BF)

    vf[me] = masked_rows(vg_ref, vm_ref)
    of[me] = masked_rows(og_ref, om_ref)
    pl.semaphore_wait(barrier, n - 1)

    def send_small(peer):
        for i, ref in enumerate((vf, of)):
            pltpu.make_async_remote_copy(
                ref.at[me], ref.at[me], small_send.at[i], small_recv.at[i], **target(peer)
            ).start()

    each_peer(send_small)

    for a in range(row_atoms):
        factor[a] = factors(tmask_ref[:, a, :])
    src = lax.broadcasted_iota(jnp.int32, (wide, wide), 0)
    dst = lax.broadcasted_iota(jnp.int32, (wide, wide), 1)
    same = (src // LANES == (dst % LANES) // width) & ((src % LANES) // width == dst // LANES)
    perm[...] = one_hot(same & (src % width == dst % width)).astype(BF)
    load.wait()

    def shuffle(parts, out, q):
        stacked = jnp.concatenate(
            [
                jnp.concatenate([x[:, c * LANES : (c + 1) * LANES] for x in parts], axis=1)
                for c in range(chunks)
            ],
            axis=0,
        )
        moved = jnp.dot(stacked, perm[...], preferred_element_type=F32).astype(BF)
        for c in range(chunks):
            for i in range(pack):
                piece = moved[
                    c * block_rows : (c + 1) * block_rows, i * LANES : (i + 1) * LANES
                ]
                out[c * pack + i, pl.ds(q * GROUPS, GROUPS)] = piece.reshape(GROUPS, width, LANES)

    def send_step(out, into, q, send_sem, recv_sem):
        here = pl.ds(q * GROUPS, GROUPS)

        def send(peer):
            pltpu.make_async_remote_copy(
                out.at[peer, here], into.at[me, here], send_sem, recv_sem, **target(peer)
            ).start()

        each_peer(send)

    def tensor_step(q, carry):
        parts = []
        for j in range(pack):
            rows = []
            for r in range(GROUPS):
                p = j * groups + q * GROUPS + r
                f = [factor[a, pl.ds(p, 1), :] * live_rows[a] for a in range(row_atoms)]
                value = (tm[p].astype(F32) * jnp.concatenate(f, axis=0)).astype(BF)
                tm[p] = value
                rows.append(value)
            parts.append(jnp.concatenate(rows, axis=0))
        shuffle(parts, st, q)
        send_step(st, rt, q, t_send, t_recv)
        return carry

    lax.fori_loop(0, steps, tensor_step, 0)
    own_t = pltpu.make_async_copy(st.at[me], rt.at[me], own_sem.at[0])
    own_t.start()

    wait_for(vf.at[pl.ds(0, n - 1)], small_recv.at[0])
    vt[...] = vf[...].reshape(basis, basis).T

    def half_step(q, carry):
        rows = [
            tm[pl.ds(j * groups + q * GROUPS, GROUPS)].reshape(block_rows, basis)
            for j in range(pack)
        ]
        half = jnp.dot(
            jnp.concatenate(rows, axis=0), vt[...], preferred_element_type=F32
        ).astype(BF)
        shuffle([half[j * block_rows : (j + 1) * block_rows] for j in range(pack)], sh, q)
        send_step(sh, rh, q, h_send, h_recv.at[q])
        return carry

    lax.fori_loop(0, steps, half_step, 0)
    own_h = pltpu.make_async_copy(sh.at[me], rh.at[me], own_sem.at[1])
    own_h.start()

    slot = lax.broadcasted_iota(jnp.int32, (n * pad_rows, aux), 0)
    wanted = jnp.where(slot % pad_rows < owned, (slot // pad_rows) * owned + slot % pad_rows, -1)
    by_p = one_hot(wanted == owner_ref[...]).astype(BF)
    p_row = lax.broadcasted_iota(jnp.int32, (aux, aux), 0)
    p_col = lax.broadcasted_iota(jnp.int32, (aux, aux), 1)
    reorder = one_hot(p_row == (p_col % pack) * groups + p_col // pack).astype(BF)
    route[...] = jnp.dot(by_p, reorder, preferred_element_type=F32)
    chi[...] = jnp.zeros_like(chi)

    wait_for(of.at[pl.ds(0, n - 1)], small_recv.at[1])
    own_t.wait()
    wait_for(rt.at[pl.ds(0, n - 1)], t_recv)

    def turn(g, carry):
        tm[pl.ds(g * pack, pack)] = rt[:, g].reshape(basis, LANES).T.reshape(pack, width, basis)
        return carry

    lax.fori_loop(0, groups, turn, 0)
    own_h.wait()

    lanes = GROUPS * LANES
    diag = one_hot(
        lax.broadcasted_iota(jnp.int32, (width, lanes), 0)
        == lax.broadcasted_iota(jnp.int32, (width, lanes), 1) % width
    )
    b_row = lax.broadcasted_iota(jnp.int32, (lanes, chi.shape[1]), 0)
    b_col = lax.broadcasted_iota(jnp.int32, (lanes, chi.shape[1]), 1)
    place = (b_row % LANES) // width * groups + b_row // LANES

    def chi_step(q, carry):
        here = pl.ds(q * GROUPS, GROUPS)
        wait_for(rh.at[pl.ds(0, n - 1), here], h_recv.at[q])
        half = jnp.concatenate(
            [rh[:, q * GROUPS + r].reshape(basis, LANES) for r in range(GROUPS)], axis=1
        )
        response = jnp.dot(
            of[...].reshape(basis, basis), half, preferred_element_type=F32
        ).astype(BF)
        gather = one_hot(b_col == place + q * GROUPS)

        tile = GROUPS * pack
        for t in range(steps):
            left = tm[t * tile : (t + 1) * tile].reshape(tile * width, basis)
            both = jnp.dot(left, response, preferred_element_type=F32)
            traced = jnp.sum(both.reshape(tile, width, lanes) * diag[None], axis=1)
            chi[t * tile : (t + 1) * tile, :] += jnp.dot(
                traced, gather, precision=lax.Precision.HIGHEST, preferred_element_type=F32
            )
        return carry

    lax.fori_loop(0, steps, chi_step, 0)

    routed = jnp.dot(
        route[...], chi[...], precision=lax.Precision.HIGHEST, preferred_element_type=F32
    )
    csend[...] = routed.reshape(csend.shape)
    crecv[me] = csend[me]

    def send_chi(peer):
        pltpu.make_async_remote_copy(
            csend.at[peer], crecv.at[me], c_send, c_recv, **target(peer)
        ).start()

    each_peer(send_chi)
    wait_for(crecv.at[pl.ds(0, n - 1)], c_recv)
    total = jnp.sum(crecv[...], axis=0) * (1.0 / basis)
    out_ref[...] = total[:owned, :aux]

    wait_for(vf.at[pl.ds(0, n - 1)], small_send.at[0])
    wait_for(of.at[pl.ds(0, n - 1)], small_send.at[1])
    wait_for(st.at[pl.ds(0, n - 1)], t_send)
    wait_for(sh.at[pl.ds(0, n - 1)], h_send)
    wait_for(csend.at[pl.ds(0, n - 1)], c_send)


def local(
    n,
    three_center,
    tensor_mask,
    occupied_green,
    occupied_mask,
    virtual_green,
    virtual_mask,
    atom_size,
    auxiliary_owner,
):
    aux, width, basis = three_center.shape
    pack = LANES // width
    groups = aux // pack
    steps = groups // GROUPS
    wide = pack * LANES
    owned = aux // n
    pad_rows = -(-owned // 8) * 8
    cols = -(-aux // LANES) * LANES
    vmem = pl.BlockSpec(memory_space=pltpu.VMEM)
    exchanged = (n, groups, width, LANES)
    dma = pltpu.SemaphoreType.DMA
    return pl.pallas_call(
        functools.partial(kernel, n),
        out_shape=jax.ShapeDtypeStruct((owned, aux), F32),
        in_specs=[pl.BlockSpec(memory_space=pl.ANY)]
        + [vmem] * 5
        + [pl.BlockSpec(memory_space=pltpu.SMEM), vmem],
        out_specs=vmem,
        scratch_shapes=[
            pltpu.VMEM((aux, width, basis), BF),
            pltpu.VMEM(exchanged, BF),
            pltpu.VMEM(exchanged, BF),
            pltpu.VMEM(exchanged, BF),
            pltpu.VMEM(exchanged, BF),
            pltpu.VMEM((n, width, basis), BF),
            pltpu.VMEM((n, width, basis), BF),
            pltpu.VMEM((basis, basis), BF),
            pltpu.VMEM((wide, wide), BF),
            pltpu.VMEM((width // FA, aux, basis), F32),
            pltpu.VMEM((aux, cols), F32),
            pltpu.VMEM((n * pad_rows, aux), F32),
            pltpu.VMEM((n, pad_rows, cols), F32),
            pltpu.VMEM((n, pad_rows, cols), F32),
            dma,
            dma((2,)),
            dma((2,)),
            dma((2,)),
            dma,
            dma,
            dma,
            dma((steps,)),
            dma,
            dma,
        ],
        compiler_params=pltpu.CompilerParams(
            collective_id=0, has_side_effects=True, vmem_limit_bytes=60 * 1024 * 1024
        ),
    )(
        three_center,
        tensor_mask,
        occupied_green,
        occupied_mask,
        virtual_green,
        virtual_mask,
        atom_size,
        auxiliary_owner.reshape(1, aux),
    )


def solution(mesh):
    placed = (
        P(None, "basis", None),
        P(None, "basis", None),
        P(("tau", "basis"), None),
        P(("tau", "basis"), None),
        P(("tau", "basis"), None),
        P(("tau", "basis"), None),
        P(),
        P(),
    )
    return jax.shard_map(
        functools.partial(local, mesh.shape["basis"]),
        mesh=mesh,
        in_specs=placed,
        out_specs=P(("tau", "basis"), None),
        check_vma=False,
    )
```

time: 232 us -> 132 us (0.57)
  blocking collectives: 147 us -> 0 us
  Pallas kernels: 0 us -> 129 us
  waiting for transfers between devices: 35.6 us -> 0 us
  local copies, waits for them, and re-layouts: 26.1 us -> 2.69 us
  starting transfers between devices: 11.2 us -> 0 us
  other arithmetic: 6.47 us -> 0 us
  matrix products: 4.65 us -> 0 us
    pallas_call x0 -> x1, Pallas kernels: none -> 129 us  [local(): pl.pallas_call(functools.partial(kernel, n), out_shape=jax.ShapeDtypeStru...]
    all_gather x2 -> x0, blocking collectives: 79.5 us -> none  [the longest x1 55.5 us: local(): lax.all_gather(occupied, 'basis', axis=0, tiled=True)]
    unnamed x1 -> x0, blocking collectives: 67.2 us -> none
    all_to_all x2 -> x0, waiting for transfers between devices: 35.6 us -> none  [the longest x1 35.6 us: local(): lax.all_to_all(response_slab, 'basis', split_axis=1, concat_axis=0, tiled...]
    all_to_all x2 -> x0, starting transfers between devices: 11.2 us -> none  [the longest x1 7.53 us: local(): lax.all_to_all(ordered, 'basis', split_axis=0, concat_axis=1, tiled=True)]
    mul x8 -> x0, local copies, waits for them, and re-layouts: 9 us -> none  [the longest x7 8.35 us: expand_factor(): block_mask.astype(jnp.bfloat16)[..., :, None, :, None]]
    dot_general x2 -> x0, matrix products: 4.65 us -> none  [the longest x1 3.96 us: local(): jnp.einsum('mn,pnl->pml', lax.all_gather(occupied, 'basis', axis=0, tiled...]
    unnamed x18 -> x2, local copies, waits for them, and re-layouts: 6.36 us -> 2.69 us
  transfers between devices with their start and end apart: 2 -> 0, of which waited for: 1 -> 0; matrix products, arithmetic and copies ran while one was open for 3% -> 0% of each run, Pallas kernels for 0% -> 0%
where the time goes in v1:
time: 132 us
  Pallas kernels  129 us (98%)
  local copies, waits for them, and re-layouts  2.69 us (2%)
    pallas_call x1, Pallas kernels, local(): pl.pallas_call(functools.partial(kernel, n), out_shape=jax.ShapeDtypeStru...  129 us
    unnamed x2, local copies, waits for them, and re-layouts  2.69 us

profile of v1, /device:TPU:0, one launch (start us, length us, event | category | flops | bytes accessed | tf_op | source)
XLA Modules:
  0.0 131.8 jit_solution(15274090125775126651)
XLA Ops:
  0.0 1.5 %copy.9.tmask_ref = s32[64,2,32]{2,1,0:T(2,128)} copy(s32[64,2,32]{0,2,1:T(8,128)} %param.9) | data formatting | bytes 32768 | tf_op args[1]
  1.5 129.1 %shard_map.82 = f32[4,64]{1,0:T(4,128)} custom-call(bf16[64,32,512]{2,1,0:T(8,128)(2,1)} %t_hbm.1, s32[64,2,32]{2,1,0:T(2,128)} %copy.9.tmask_ref, bf16[32,512]{1,0:T(8,128)(2,1)} %og_ref.1, s32[2,32]{1,0:T(2,128)} %om_ref.1, bf16[32,512]{1,0:T(8,128)(2,1)} %vg_ref.1, s32[2,32]{1,0:T(2,128)} %vm_ref.1, s32[32]{0:T(128)} %size_ref.1, s32[1,64]{1,0:T(1,128)} %bitcast.1), custom_call_target="tpu_custom_call" | custom-call | tf_op jit(solution)/shard_map/pallas_call | solution.py:296
  130.6 1.2 copy.11

commit v2 on v1

v2 whole, which is shorter than its diff:
```python
import functools

import jax
import jax.numpy as jnp
from jax import lax
from jax.experimental import pallas as pl
from jax.experimental.pallas import tpu as pltpu
from jax.sharding import PartitionSpec as P

FA = 16
LANES = 128
GROUPS = 2
BF = jnp.bfloat16
F32 = jnp.float32


def wait_for(ref, sem):
    pltpu.make_async_copy(ref, ref, sem).wait()


def one_hot(cond):
    return jnp.where(cond, 1.0, 0.0).astype(F32)


def kernel(
    n,
    parts,
    t_hbm,
    tmask_ref,
    og_ref,
    om_ref,
    vg_ref,
    vm_ref,
    size_ref,
    owner_ref,
    out_ref,
    tm,
    st,
    sh,
    rt,
    rh,
    vown,
    vf,
    of,
    vt,
    perm_t,
    perm_h,
    factor,
    chi,
    route,
    csend,
    crecv,
    cmine,
    cother,
    load_sem,
    own_sem,
    v_send,
    v_recv,
    o_send,
    o_recv,
    t_send,
    t_recv,
    h_send,
    h_recv,
    c_send,
    c_recv,
):
    me = lax.axis_index("basis")
    tau = lax.axis_index("tau")
    aux, width, basis = tm.shape
    share = width // parts
    pack = LANES // share
    groups = aux // pack
    steps = groups // GROUPS
    atoms = basis // FA
    row_atoms = width // FA
    rows = GROUPS * width
    owned = aux // n
    high = n // 4
    h_me, m_me, c_me = me // 4, (me // 2) % 2, me % 2

    def peer_of(k):
        return lax.rem(me + k, n)

    def each_peer(body):
        def step(k, carry):
            body(peer_of(k))
            return carry

        lax.fori_loop(1, n, step, 0)

    def at(part, place):
        return dict(device_id=(part, place), device_id_type=pl.DeviceIdType.MESH)

    def send(src, dst, send_sem, recv_sem, part, place):
        pltpu.make_async_remote_copy(src, dst, send_sem, recv_sem, **at(part, place)).start()

    other_parts = [lax.rem(tau + k, parts) for k in range(1, parts)]

    barrier = pltpu.get_barrier_semaphore()
    each_peer(lambda peer: pl.semaphore_signal(barrier, inc=1, **at(tau, peer)))
    for part in other_parts:
        pl.semaphore_signal(barrier, inc=1, **at(part, me))
    load = pltpu.make_async_copy(t_hbm, tm, load_sem)
    load.start()

    lane = lax.broadcasted_iota(jnp.int32, (1, basis), 1)
    live = jnp.zeros((1, basis), F32)
    for a in range(atoms):
        hit = (lane >= a * FA) & (lane < a * FA + size_ref[a])
        live = live + one_hot(hit)
    atom_row = lax.broadcasted_iota(jnp.int32, (atoms, basis), 0)
    atom_lane = lax.broadcasted_iota(jnp.int32, (atoms, basis), 1) // FA
    spread = (one_hot(atom_row == atom_lane) * live).astype(BF)
    within = lax.broadcasted_iota(jnp.int32, (FA, basis), 0)
    live_rows = [one_hot(within < size_ref[me * row_atoms + a]) for a in range(row_atoms)]

    def factors(mask):
        return jnp.dot(mask.astype(F32).astype(BF), spread, preferred_element_type=F32)

    def masked_rows(rows_ref, mask_ref):
        f = factors(mask_ref[...])
        return jnp.concatenate(
            [
                rows_ref[a * FA : (a + 1) * FA, :].astype(F32) * (f[a : a + 1, :] * live_rows[a])
                for a in range(row_atoms)
            ],
            axis=0,
        )

    virtual = masked_rows(vg_ref, vm_ref)
    for x in range(parts):
        vown[x] = virtual[x * share : (x + 1) * share].astype(BF)
    vf[h_me, m_me, c_me, tau] = vown[tau]
    of[tau, h_me, m_me, c_me] = masked_rows(og_ref, om_ref).astype(BF)
    pl.semaphore_wait(barrier, n - 1 + parts - 1)

    def across(k, block, send_sem, recv_sem):
        hi = lax.rem(h_me + k, high)
        send(block, block, send_sem, recv_sem, tau, hi * 4 + m_me * 2 + c_me)

    mid_partner = h_me * 4 + (1 - m_me) * 2 + c_me
    core_partner = h_me * 4 + m_me * 2 + (1 - c_me)

    for part in other_parts:
        send(vown.at[part], vf.at[h_me, m_me, c_me, tau], v_send.at[0], v_recv.at[0], part, me)
    v_block = vf.at[h_me, m_me, c_me]
    o_block = of.at[tau, h_me, m_me, c_me]
    for k in range(1, high):
        across(k, o_block, o_send.at[0], o_recv.at[0])

    for a in range(row_atoms):
        factor[a] = factors(tmask_ref[:, a, :])

    def fill(table, piece, offset):
        count = table.shape[1]
        dst = lax.broadcasted_iota(jnp.int32, (1, count), 1)
        from_lane = (dst // LANES) * piece + dst % share + offset
        member = (dst % LANES) // share
        src = lax.broadcasted_iota(jnp.int32, (LANES, count), 0)
        for j in range(pack):
            wanted_lane = jnp.where(member == j, from_lane, -1)
            table[j * LANES : (j + 1) * LANES, :] = one_hot(src == wanted_lane).astype(BF)

    fill(perm_t, width, tau * share)

    def wait_v(stage, ref):
        wait_for(ref, v_recv.at[stage])

    wait_v(0, vown.at[pl.ds(0, parts - 1)])
    for k in range(1, high):
        across(k, v_block, v_send.at[1], v_recv.at[1])
    load.wait()

    def stack(pieces):
        chunks = pieces[0].shape[1] // LANES
        return jnp.concatenate(
            [
                jnp.concatenate([x[:, c * LANES : (c + 1) * LANES] for x in pieces], axis=1)
                for c in range(chunks)
            ],
            axis=0,
        )

    def tensor_step(q, carry):
        pieces = []
        for j in range(pack):
            values = []
            for r in range(GROUPS):
                p = j * groups + q * GROUPS + r
                f = [factor[a, pl.ds(p, 1), :] * live_rows[a] for a in range(row_atoms)]
                value = (tm[p].astype(F32) * jnp.concatenate(f, axis=0)).astype(BF)
                tm[p] = value
                values.append(value)
            pieces.append(jnp.concatenate(values, axis=0))
        moved = jnp.dot(stack(pieces), perm_t[...], preferred_element_type=F32).astype(BF)
        here = pl.ds(q * GROUPS, GROUPS)
        per = LANES // width
        for c in range(basis // LANES):
            for i in range(per):
                piece = moved[c * rows : (c + 1) * rows, i * LANES : (i + 1) * LANES]
                st[c * per + i, here] = piece.reshape(GROUPS, width, LANES)
        each_peer(
            lambda peer: send(st.at[peer, here], rt.at[me, here], t_send, t_recv, tau, peer)
        )
        return carry

    lax.fori_loop(0, 1, tensor_step, 0)
    wait_v(1, vf.at[pl.ds(0, high - 1), 0, 0])
    v_line = vf.at[:, m_me, c_me]
    send(v_line, v_line, v_send.at[2], v_recv.at[2], tau, mid_partner)
    wait_for(of.at[0, pl.ds(0, high - 1), 0, 0], o_recv.at[0])
    o_line = of.at[tau, :, m_me, c_me]
    send(o_line, o_line, o_send.at[1], o_recv.at[1], tau, mid_partner)

    lax.fori_loop(1, 2, tensor_step, 0)
    wait_v(2, v_line)
    v_plane = vf.at[:, :, c_me]
    send(v_plane, v_plane, v_send.at[3], v_recv.at[3], tau, core_partner)
    wait_for(o_line, o_recv.at[1])
    o_plane = of.at[tau, :, :, c_me]
    send(o_plane, o_plane, o_send.at[2], o_recv.at[2], tau, core_partner)

    lax.fori_loop(2, steps, tensor_step, 0)
    own_t = pltpu.make_async_copy(st.at[me], rt.at[me], own_sem.at[0])
    own_t.start()
    fill(perm_h, share, 0)

    wait_for(o_plane, o_recv.at[2])
    for part in other_parts:
        send(of.at[tau], of.at[tau], o_send.at[3], o_recv.at[3], part, me)
    wait_v(3, v_plane)
    mine = n * share
    for t in range(parts):
        vt[:, t * mine : (t + 1) * mine] = vf[:, :, :, t].reshape(mine, basis).T

    def half_step(q, carry):
        here = pl.ds(q * GROUPS, GROUPS)
        left = [
            tm[pl.ds(j * groups + q * GROUPS, GROUPS)].reshape(rows, basis) for j in range(pack)
        ]
        half = jnp.dot(
            jnp.concatenate(left, axis=0), vt[...], preferred_element_type=F32
        ).astype(BF)
        pieces = [half[j * rows : (j + 1) * rows] for j in range(pack)]
        moved = jnp.dot(stack(pieces), perm_h[...], preferred_element_type=F32).astype(BF)
        for c in range(basis // LANES):
            for i in range(pack):
                t, e = divmod(c * pack + i, n)
                piece = moved[c * rows : (c + 1) * rows, i * LANES : (i + 1) * LANES]
                sh[e, here, t] = piece.reshape(GROUPS, width, LANES)
        each_peer(
            lambda peer: send(sh.at[peer, here], rh.at[me, here], h_send, h_recv.at[q], tau, peer)
        )
        return carry

    lax.fori_loop(0, steps, half_step, 0)
    own_h = pltpu.make_async_copy(sh.at[me], rh.at[me], own_sem.at[1])
    own_h.start()

    pad_rows = csend.shape[1]
    slot = lax.broadcasted_iota(jnp.int32, (n * pad_rows, aux), 0)
    wanted = jnp.where(slot % pad_rows < owned, (slot // pad_rows) * owned + slot % pad_rows, -1)
    by_p = one_hot(wanted == owner_ref[...]).astype(BF)
    p_row = lax.broadcasted_iota(jnp.int32, (aux, aux), 0)
    p_col = lax.broadcasted_iota(jnp.int32, (aux, aux), 1)
    reorder = one_hot(p_row == (p_col % pack) * groups + p_col // pack).astype(BF)
    route[...] = jnp.dot(by_p, reorder, preferred_element_type=F32)
    chi[...] = jnp.zeros_like(chi)

    own_t.wait()
    wait_for(rt.at[pl.ds(0, n - 1)], t_recv)
    tiles = LANES // width

    def turn(g, carry):
        turned = rt[:, g].reshape(basis, LANES).T
        tm[pl.ds(g * tiles, tiles)] = turned.reshape(tiles, width, basis)
        return carry

    lax.fori_loop(0, groups, turn, 0)
    own_h.wait()
    wait_for(of.at[pl.ds(0, parts - 1)], o_recv.at[3])

    lanes = parts * GROUPS * LANES
    diag = one_hot(
        lax.broadcasted_iota(jnp.int32, (share, lanes), 0)
        == lax.broadcasted_iota(jnp.int32, (share, lanes), 1) % share
    )
    b_row = lax.broadcasted_iota(jnp.int32, (lanes, chi.shape[1]), 0)
    b_col = lax.broadcasted_iota(jnp.int32, (lanes, chi.shape[1]), 1)
    place = (
        b_row // (GROUPS * LANES) * aux
        + (b_row % LANES) // share * groups
        + (b_row // LANES) % GROUPS
    )

    def chi_step(q, carry):
        here = pl.ds(q * GROUPS, GROUPS)
        wait_for(rh.at[pl.ds(0, n - 1), here], h_recv.at[q])
        responses = []
        for t in range(parts):
            half = jnp.concatenate(
                [rh[:, q * GROUPS + r, t].reshape(basis, LANES) for r in range(GROUPS)], axis=1
            )
            responses.append(
                jnp.dot(
                    of[t].reshape(basis, basis), half, preferred_element_type=F32
                ).astype(BF)
            )
        response = jnp.concatenate(responses, axis=1)
        gather = one_hot(b_col == place + q * GROUPS)
        tile = 4 * tiles
        chi_rows = tile * width // share
        for k in range(groups // 4):
            left = tm[k * tile : (k + 1) * tile].reshape(tile * width, basis)
            both = jnp.dot(left, response, preferred_element_type=F32)
            traced = jnp.sum(both.reshape(chi_rows, share, lanes) * diag[None], axis=1)
            chi[k * chi_rows : (k + 1) * chi_rows, :] += jnp.dot(
                traced, gather, precision=lax.Precision.HIGHEST, preferred_element_type=F32
            )
        return carry

    lax.fori_loop(0, steps, chi_step, 0)

    routed = jnp.dot(
        route[...], chi[...], precision=lax.Precision.HIGHEST, preferred_element_type=F32
    )
    csend[...] = routed.reshape(csend.shape)
    crecv[me] = csend[me]
    each_peer(
        lambda peer: send(csend.at[peer], crecv.at[me], c_send.at[0], c_recv.at[0], tau, peer)
    )
    wait_for(crecv.at[pl.ds(0, n - 1)], c_recv.at[0])
    total = jnp.sum(crecv[...], axis=0) * (1.0 / basis)
    for t in range(parts):
        cmine[t, :, 0:aux] = total[:, t * aux : (t + 1) * aux]
    cother[tau] = cmine[tau]
    for part in other_parts:
        send(cmine.at[part], cother.at[tau], c_send.at[1], c_recv.at[1], part, me)
    wait_for(cother.at[pl.ds(0, parts - 1)], c_recv.at[1])
    out_ref[...] = jnp.sum(cother[...], axis=0)[:owned, :aux]

    wait_for(vown.at[pl.ds(0, parts - 1)], v_send.at[0])
    wait_for(vf.at[pl.ds(0, high - 1), 0, 0], v_send.at[1])
    wait_for(v_line, v_send.at[2])
    wait_for(v_plane, v_send.at[3])
    wait_for(of.at[0, pl.ds(0, high - 1), 0, 0], o_send.at[0])
    wait_for(o_line, o_send.at[1])
    wait_for(o_plane, o_send.at[2])
    wait_for(of.at[pl.ds(0, parts - 1)], o_send.at[3])
    wait_for(st.at[pl.ds(0, n - 1)], t_send)
    wait_for(sh.at[pl.ds(0, n - 1)], h_send)
    wait_for(csend.at[pl.ds(0, n - 1)], c_send.at[0])
    wait_for(cmine.at[pl.ds(0, parts - 1)], c_send.at[1])


def local(
    n,
    parts,
    three_center,
    tensor_mask,
    occupied_green,
    occupied_mask,
    virtual_green,
    virtual_mask,
    atom_size,
    auxiliary_owner,
):
    aux, width, basis = three_center.shape
    share = width // parts
    pack = LANES // share
    groups = aux // pack
    steps = groups // GROUPS
    wide = pack * LANES
    owned = aux // n
    pad_rows = -(-owned // 8) * 8
    cols = -(-parts * aux // LANES) * LANES
    one_cols = -(-aux // LANES) * LANES
    vmem = pl.BlockSpec(memory_space=pltpu.VMEM)
    sent_t = (n, groups, width, LANES)
    sent_h = (n, groups, parts, width, LANES)
    dma = pltpu.SemaphoreType.DMA
    return pl.pallas_call(
        functools.partial(kernel, n, parts),
        out_shape=jax.ShapeDtypeStruct((owned, aux), F32),
        in_specs=[pl.BlockSpec(memory_space=pl.ANY)]
        + [vmem] * 5
        + [pl.BlockSpec(memory_space=pltpu.SMEM), vmem],
        out_specs=vmem,
        scratch_shapes=[
            pltpu.VMEM((aux, width, basis), BF),
            pltpu.VMEM(sent_t, BF),
            pltpu.VMEM(sent_h, BF),
            pltpu.VMEM(sent_t, BF),
            pltpu.VMEM(sent_h, BF),
            pltpu.VMEM((parts, share, basis), BF),
            pltpu.VMEM((n // 4, 2, 2, parts, share, basis), BF),
            pltpu.VMEM((parts, n // 4, 2, 2, width, basis), BF),
            pltpu.VMEM((basis, basis), BF),
            pltpu.VMEM((wide, LANES // width * LANES), BF),
            pltpu.VMEM((wide, wide), BF),
            pltpu.VMEM((width // FA, aux, basis), F32),
            pltpu.VMEM((aux, cols), F32),
            pltpu.VMEM((n * pad_rows, aux), F32),
            pltpu.VMEM((n, pad_rows, cols), F32),
            pltpu.VMEM((n, pad_rows, cols), F32),
            pltpu.VMEM((parts, pad_rows, one_cols), F32),
            pltpu.VMEM((parts, pad_rows, one_cols), F32),
            dma,
            dma((2,)),
            dma((4,)),
            dma((4,)),
            dma((4,)),
            dma((4,)),
            dma,
            dma,
            dma,
            dma((steps,)),
            dma((2,)),
            dma((2,)),
        ],
        compiler_params=pltpu.CompilerParams(
            collective_id=0, has_side_effects=True, vmem_limit_bytes=61 * 1024 * 1024
        ),
    )(
        three_center,
        tensor_mask,
        occupied_green,
        occupied_mask,
        virtual_green,
        virtual_mask,
        atom_size,
        auxiliary_owner.reshape(1, aux),
    )


def solution(mesh):
    placed = (
        P(None, "basis", None),
        P(None, "basis", None),
        P(("tau", "basis"), None),
        P(("tau", "basis"), None),
        P(("tau", "basis"), None),
        P(("tau", "basis"), None),
        P(),
        P(),
    )
    return jax.shard_map(
        functools.partial(local, mesh.shape["basis"], mesh.shape["tau"]),
        mesh=mesh,
        in_specs=placed,
        out_specs=P(("tau", "basis"), None),
        check_vma=False,
    )
```

time: 132 us -> 98.4 us (0.75)
  Pallas kernels: 129 us -> 95.4 us
    pallas_call x1, Pallas kernels: 129 us -> 95.4 us  [local(): pl.pallas_call(functools.partial(kernel, n, parts), out_shape=jax.ShapeDt...]
where the time goes in v2:
time: 98.4 us; the launch traced here: 98.1 us
  Pallas kernels  95.4 us (97%)
  local copies, waits for them, and re-layouts  2.69 us (3%)
    pallas_call x1, Pallas kernels, local(): pl.pallas_call(functools.partial(kernel, n, parts), out_shape=jax.ShapeDt...  95.4 us
    unnamed x2, local copies, waits for them, and re-layouts  2.69 us

profile of v2, /device:TPU:0, one launch (start us, length us, event | category | flops | bytes accessed | tf_op | source)
XLA Modules:
  0.0 98.1 jit_solution(11713926190773404856)
XLA Ops:
  0.0 1.5 %copy.9.tmask_ref = s32[64,2,32]{2,1,0:T(2,128)} copy(s32[64,2,32]{0,2,1:T(8,128)} %param.9) | data formatting | bytes 32768 | tf_op args[1]
  1.5 95.4 %shard_map.82 = f32[4,64]{1,0:T(4,128)} custom-call(bf16[64,32,512]{2,1,0:T(8,128)(2,1)} %t_hbm.1, s32[64,2,32]{2,1,0:T(2,128)} %copy.9.tmask_ref, bf16[32,512]{1,0:T(8,128)(2,1)} %og_ref.1, s32[2,32]{1,0:T(2,128)} %om_ref.1, bf16[32,512]{1,0:T(8,128)(2,1)} %vg_ref.1, s32[2,32]{1,0:T(2,128)} %vm_ref.1, s32[32]{0:T(128)} %size_ref.1, s32[1,64]{1,0:T(1,128)} %bitcast.1), custom_call_target="tpu_custom_call" | custom-call | tf_op jit(solution)/shard_map/pallas_call | solution.py:383
  96.9 1.2 %copy.11 = f32[4,64]{1,0:T(4,128)} copy(f32[4,64]{1,0:T(4,128)} %shard_map.82) | data formatting | bytes 2048

commit v3 on v2

--- a/solution.py
+++ b/solution.py
@@ -77,10 +77,10 @@
     rows = GROUPS * width
     owned = aux // n
     high = n // 4
-    h_me, m_me, c_me = me // 4, (me // 2) % 2, me % 2
+    h_me, l_me = me // 4, me % 4
 
     def peer_of(k):
-        return lax.rem(me + k, n)
+        return lax.rem(me + n - k, n)
 
     def each_peer(body):
         def step(k, carry):
@@ -97,10 +97,17 @@
 
     other_parts = [lax.rem(tau + k, parts) for k in range(1, parts)]
 
+    def line_place(k):
+        return lax.rem(h_me + k, high) * 4 + l_me
+
+    line = [(part, line_place(k)) for part in other_parts for k in range(high)]
+    line += [(tau, line_place(k)) for k in range(1, high)]
+    layer = [h_me * 4 + lax.rem(me + k, 4) for k in range(1, 4)]
+
     barrier = pltpu.get_barrier_semaphore()
     each_peer(lambda peer: pl.semaphore_signal(barrier, inc=1, **at(tau, peer)))
-    for part in other_parts:
-        pl.semaphore_signal(barrier, inc=1, **at(part, me))
+    for part, place in line[: (parts - 1) * high]:
+        pl.semaphore_signal(barrier, inc=1, **at(part, place))
     load = pltpu.make_async_copy(t_hbm, tm, load_sem)
     load.start()
 
@@ -131,23 +138,16 @@
     virtual = masked_rows(vg_ref, vm_ref)
     for x in range(parts):
         vown[x] = virtual[x * share : (x + 1) * share].astype(BF)
-    vf[h_me, m_me, c_me, tau] = vown[tau]
-    of[tau, h_me, m_me, c_me] = masked_rows(og_ref, om_ref).astype(BF)
-    pl.semaphore_wait(barrier, n - 1 + parts - 1)
-
-    def across(k, block, send_sem, recv_sem):
-        hi = lax.rem(h_me + k, high)
-        send(block, block, send_sem, recv_sem, tau, hi * 4 + m_me * 2 + c_me)
-
-    mid_partner = h_me * 4 + (1 - m_me) * 2 + c_me
-    core_partner = h_me * 4 + m_me * 2 + (1 - c_me)
-
-    for part in other_parts:
-        send(vown.at[part], vf.at[h_me, m_me, c_me, tau], v_send.at[0], v_recv.at[0], part, me)
-    v_block = vf.at[h_me, m_me, c_me]
-    o_block = of.at[tau, h_me, m_me, c_me]
-    for k in range(1, high):
-        across(k, o_block, o_send.at[0], o_recv.at[0])
+    vf[l_me, h_me * parts + tau] = vown[tau]
+    of[tau, l_me, h_me] = masked_rows(og_ref, om_ref).astype(BF)
+    pl.semaphore_wait(barrier, n - 1 + (parts - 1) * high)
+
+    v_block = vf.at[l_me, h_me * parts + tau]
+    for part, place in line:
+        send(vown.at[part], v_block, v_send.at[0], v_recv.at[0], part, place)
+    o_block = of.at[tau, l_me, h_me]
+    for part, place in line[(parts - 1) * high :]:
+        send(o_block, o_block, o_send.at[0], o_recv.at[0], part, place)
 
     for a in range(row_atoms):
         factor[a] = factors(tmask_ref[:, a, :])
@@ -164,12 +164,6 @@
 
     fill(perm_t, width, tau * share)
 
-    def wait_v(stage, ref):
-        wait_for(ref, v_recv.at[stage])
-
-    wait_v(0, vown.at[pl.ds(0, parts - 1)])
-    for k in range(1, high):
-        across(k, v_block, v_send.at[1], v_recv.at[1])
     load.wait()
 
     def stack(pieces):
@@ -206,33 +200,25 @@
         return carry
 
     lax.fori_loop(0, 1, tensor_step, 0)
-    wait_v(1, vf.at[pl.ds(0, high - 1), 0, 0])
-    v_line = vf.at[:, m_me, c_me]
-    send(v_line, v_line, v_send.at[2], v_recv.at[2], tau, mid_partner)
-    wait_for(of.at[0, pl.ds(0, high - 1), 0, 0], o_recv.at[0])
-    o_line = of.at[tau, :, m_me, c_me]
-    send(o_line, o_line, o_send.at[1], o_recv.at[1], tau, mid_partner)
-
-    lax.fori_loop(1, 2, tensor_step, 0)
-    wait_v(2, v_line)
-    v_plane = vf.at[:, :, c_me]
-    send(v_plane, v_plane, v_send.at[3], v_recv.at[3], tau, core_partner)
-    wait_for(o_line, o_recv.at[1])
-    o_plane = of.at[tau, :, :, c_me]
-    send(o_plane, o_plane, o_send.at[2], o_recv.at[2], tau, core_partner)
-
-    lax.fori_loop(2, steps, tensor_step, 0)
+    wait_for(vf.at[0, pl.ds(0, parts * high - 1)], v_recv.at[0])
+    v_line = vf.at[l_me]
+    for place in layer:
+        send(v_line, v_line, v_send.at[1], v_recv.at[1], tau, place)
+    wait_for(of.at[0, 0, pl.ds(0, high - 1)], o_recv.at[0])
+    o_line = of.at[tau, l_me]
+    for place in layer:
+        send(o_line, o_line, o_send.at[1], o_recv.at[1], tau, place)
+
+    lax.fori_loop(1, steps, tensor_step, 0)
     own_t = pltpu.make_async_copy(st.at[me], rt.at[me], own_sem.at[0])
     own_t.start()
     fill(perm_h, share, 0)
 
-    wait_for(o_plane, o_recv.at[2])
-    for part in other_parts:
-        send(of.at[tau], of.at[tau], o_send.at[3], o_recv.at[3], part, me)
-    wait_v(3, v_plane)
+    wait_for(vf.at[pl.ds(0, 3)], v_recv.at[1])
     mine = n * share
     for t in range(parts):
-        vt[:, t * mine : (t + 1) * mine] = vf[:, :, :, t].reshape(mine, basis).T
+        ordered = [vf[:, h * parts + t].reshape(4 * share, basis) for h in range(high)]
+        vt[:, t * mine : (t + 1) * mine] = jnp.concatenate(ordered, axis=0).T
 
     def half_step(q, carry):
         here = pl.ds(q * GROUPS, GROUPS)
@@ -257,6 +243,9 @@
     lax.fori_loop(0, steps, half_step, 0)
     own_h = pltpu.make_async_copy(sh.at[me], rh.at[me], own_sem.at[1])
     own_h.start()
+    wait_for(of.at[0, pl.ds(0, 3)], o_recv.at[1])
+    for part in other_parts:
+        send(of.at[tau], of.at[tau], o_send.at[2], o_recv.at[2], part, me)
 
     pad_rows = csend.shape[1]
     slot = lax.broadcasted_iota(jnp.int32, (n * pad_rows, aux), 0)
@@ -279,7 +268,7 @@
 
     lax.fori_loop(0, groups, turn, 0)
     own_h.wait()
-    wait_for(of.at[pl.ds(0, parts - 1)], o_recv.at[3])
+    wait_for(of.at[pl.ds(0, parts - 1)], o_recv.at[2])
 
     lanes = parts * GROUPS * LANES
     diag = one_hot(
@@ -302,10 +291,11 @@
             half = jnp.concatenate(
                 [rh[:, q * GROUPS + r, t].reshape(basis, LANES) for r in range(GROUPS)], axis=1
             )
+            occupied = jnp.concatenate(
+                [of[t, :, h].reshape(4 * width, basis) for h in range(high)], axis=0
+            )
             responses.append(
-                jnp.dot(
-                    of[t].reshape(basis, basis), half, preferred_element_type=F32
-                ).astype(BF)
+                jnp.dot(occupied, half, preferred_element_type=F32).astype(BF)
             )
         response = jnp.concatenate(responses, axis=1)
         gather = one_hot(b_col == place + q * GROUPS)
@@ -340,14 +330,11 @@
     wait_for(cother.at[pl.ds(0, parts - 1)], c_recv.at[1])
     out_ref[...] = jnp.sum(cother[...], axis=0)[:owned, :aux]
 
-    wait_for(vown.at[pl.ds(0, parts - 1)], v_send.at[0])
-    wait_for(vf.at[pl.ds(0, high - 1), 0, 0], v_send.at[1])
-    wait_for(v_line, v_send.at[2])
-    wait_for(v_plane, v_send.at[3])
-    wait_for(of.at[0, pl.ds(0, high - 1), 0, 0], o_send.at[0])
-    wait_for(o_line, o_send.at[1])
-    wait_for(o_plane, o_send.at[2])
-    wait_for(of.at[pl.ds(0, parts - 1)], o_send.at[3])
+    wait_for(vf.at[0, pl.ds(0, parts * high - 1)], v_send.at[0])
+    wait_for(vf.at[pl.ds(0, 3)], v_send.at[1])
+    wait_for(of.at[0, 0, pl.ds(0, high - 1)], o_send.at[0])
+    wait_for(of.at[0, pl.ds(0, 3)], o_send.at[1])
+    wait_for(of.at[pl.ds(0, parts - 1)], o_send.at[2])
     wait_for(st.at[pl.ds(0, n - 1)], t_send)
     wait_for(sh.at[pl.ds(0, n - 1)], h_send)
     wait_for(csend.at[pl.ds(0, n - 1)], c_send.at[0])
@@ -394,8 +381,8 @@
             pltpu.VMEM(sent_t, BF),
             pltpu.VMEM(sent_h, BF),
             pltpu.VMEM((parts, share, basis), BF),
-            pltpu.VMEM((n // 4, 2, 2, parts, share, basis), BF),
-            pltpu.VMEM((parts, n // 4, 2, 2, width, basis), BF),
+            pltpu.VMEM((4, n // 4 * parts, share, basis), BF),
+            pltpu.VMEM((parts, 4, n // 4, width, basis), BF),
             pltpu.VMEM((basis, basis), BF),
             pltpu.VMEM((wide, LANES // width * LANES), BF),
             pltpu.VMEM((wide, wide), BF),
@@ -408,10 +395,10 @@
             pltpu.VMEM((parts, pad_rows, one_cols), F32),
             dma,
             dma((2,)),
-            dma((4,)),
-            dma((4,)),
-            dma((4,)),
-            dma((4,)),
+            dma((2,)),
+            dma((2,)),
+            dma((3,)),
+            dma((3,)),
             dma,
             dma,
             dma,

time: 98.4 us -> 93.9 us (0.954)
  Pallas kernels: 95.4 us -> 90.9 us
    pallas_call x1, Pallas kernels: 95.4 us -> 90.9 us  [local(): pl.pallas_call(functools.partial(kernel, n, parts), out_shape=jax.ShapeDt...]
where the time goes in v3:
time: 93.9 us; the launch traced here: 93.6 us
  Pallas kernels  90.9 us (97%)
  local copies, waits for them, and re-layouts  2.69 us (3%)
    pallas_call x1, Pallas kernels, local(): pl.pallas_call(functools.partial(kernel, n, parts), out_shape=jax.ShapeDt...  90.9 us
    unnamed x2, local copies, waits for them, and re-layouts  2.69 us

profile of v3, /device:TPU:0, one launch (start us, length us, event | category | flops | bytes accessed | tf_op | source)
XLA Modules:
  0.0 93.6 jit_solution(11356101442515226001)
XLA Ops:
  0.0 1.5 %copy.9.tmask_ref = s32[64,2,32]{2,1,0:T(2,128)} copy(s32[64,2,32]{0,2,1:T(8,128)} %param.9) | data formatting | bytes 32768 | tf_op args[1]
  1.5 90.9 %shard_map.82 = f32[4,64]{1,0:T(4,128)} custom-call(bf16[64,32,512]{2,1,0:T(8,128)(2,1)} %t_hbm.1, s32[64,2,32]{2,1,0:T(2,128)} %copy.9.tmask_ref, bf16[32,512]{1,0:T(8,128)(2,1)} %og_ref.1, s32[2,32]{1,0:T(2,128)} %om_ref.1, bf16[32,512]{1,0:T(8,128)(2,1)} %vg_ref.1, s32[2,32]{1,0:T(2,128)} %vm_ref.1, s32[32]{0:T(128)} %size_ref.1, s32[1,64]{1,0:T(1,128)} %bitcast.1), custom_call_target="tpu_custom_call" | custom-call | tf_op jit(solution)/shard_map/pallas_call | solution.py:370
  92.4 1.2 %copy.11 = f32[4,64]{1,0:T(4,128)} copy(f32[4,64]{1,0:T(4,128)} %shard_map.82) | data formatting | bytes 2048
